TPU v7x, 128 devices: a whole 4x4x4 slice. The times are simulated.
128 devices in a mesh: row: 8 (over z, x_lo), col: 16 (over x_hi, y, core).
Axes of the slice: x: 4 (x_hi: 2, x_lo: 2; x = x_hi * 2 + x_lo), y: 4, z: 4, core: 2. Of those that a mesh axis runs over, the one named last changes fastest.
Arguments:
- prior: float32 [16384, 16384], P('row', 'col'), may hold values from -6 to 6, as said below
- observed: int32 [512], replicated, may hold values from 0 to 16383, as said below
- obs_noise: float32 [512], replicated, may hold values from 0.25 to 1
Outputs:
- posterior: float32 [16384, 16384], P('row', 'col')
Inputs may be any that keep to these rules, and one draw needn't show every extreme that they name: prior is symmetric positive semidefinite, and exactly symmetric: prior[i, j] equals prior[j, i] bit for bit. States may repeat; the largest and smallest states of the range are observed in every draw.
All inputs are finite; a program needn't handle non-finite values.
Results may differ from a plain program's by a relative error of at most 0.00012.
Values sent between devices are 32-bit elements; how exact they have to be, the bound alone decides.
No kernel may reach another device: no remote copies, remote signals or barrier semaphores. Data moves between devices by JAX's collectives and lax.ppermute only.
A program may use at most 128 MiB of HBM per device.

v0:
```python
import jax
import jax.numpy as jnp
from jax import lax
from jax.sharding import PartitionSpec as P


def spread(value, axis, source):
    kept = jnp.where(lax.axis_index(axis) == source, value, 0).astype(value.dtype)
    return lax.psum(kept, axis)


def local(prior, observed, obs_noise):
    rows_dev = prior.shape[0]
    cols_dev = prior.shape[1]
    row_id = lax.axis_index("row")
    col_id = lax.axis_index("col")
    row_start = row_id * rows_dev
    col_start = col_id * cols_dev
    local_col = observed - col_start
    in_col = (local_col >= 0) & (local_col < cols_dev)
    col_pick = jnp.clip(local_col, 0, cols_dev - 1)
    local_row = observed - row_start
    in_row = (local_row >= 0) & (local_row < rows_dev)
    row_pick = jnp.clip(local_row, 0, rows_dev - 1)
    partial_panel = jnp.where(in_col[None, :], jnp.take(prior, col_pick, axis=1), 0.0)
    row_panel = lax.psum(partial_panel, "col")
    per_row = rows_dev // cols_dev
    own_piece = lax.dynamic_slice_in_dim(row_panel, col_id % per_row * cols_dev, cols_dev, 0)
    col_panel = spread(own_piece, "row", col_id // per_row)
    panel_part = jnp.where(in_row[:, None], jnp.take(row_panel, row_pick, axis=0), 0.0)
    innovation = lax.psum(panel_part, "row")
    innovation = innovation + jnp.diag(obs_noise)
    factor = jnp.linalg.cholesky(innovation)
    forward = lax.linalg.triangular_solve(factor, row_panel.T, left_side=True, lower=True)
    weighted = lax.linalg.triangular_solve(
        factor, forward, left_side=True, lower=True, transpose_a=True
    )
    update = lax.dot_general(
        col_panel,
        weighted,
        (((1,), (0,)), ((), ())),
        precision=lax.Precision.HIGHEST,
        preferred_element_type=jnp.float32,
    )
    return prior - update.T


def solution(mesh):
    return jax.shard_map(
        local,
        mesh=mesh,
        in_specs=(P("row", "col"), P(), P()),
        out_specs=P("row", "col"),
        check_vma=False,
    )
```

profile of v0, /device:TPU:1, one launch (start us, length us, event | category | flops | bytes accessed | tf_op | source)
XLA Modules:
  0.0 523.1 jit_solution(11798599762217247784)
XLA Ops:
  6.5 0.7 compare_and_fusion.3
  7.2 9.1 %copy.4 = f32[2048,1024]{0,1:T(8,128)} copy(f32[2048,1024]{1,0:T(8,128)} %param.3) | data formatting | bytes 16777216 | tf_op args[0]
  16.4 8.8 %gather_fusion = f32[512,2048]{1,0:T(8,128)} fusion(f32[2048,1024]{0,1:T(8,128)} %copy.4, s32[1024]{0:T(1024)S(1)} %pad_clamp_fusion.1), kind=kCustom, calls=%fused_computation | custom fusion | bytes 8390656 | tf_op jit(solution)/shard_map/jit(_take)/gather | solution.py:25
  25.1 4.7 select_bitcast_fusion
  29.9 153.2 %all-reduce.5.cloned.1.call-done = f32[2048,512]{0,1:T(8,128)} async-done(((f32[2048,512]{0,1:T(8,128)}), f32[2048,512]{0,1:T(8,128)}) %all-reduce.5.cloned.1.call-update) | async-done | bytes 4194320 | tf_op jit(solution)/shard_map/psum | solution.py:26
  183.1 5.3 %copy.5 = f32[2048,512]{1,0:T(8,128)} copy(f32[2048,512]{0,1:T(8,128)} %all-reduce.5.cloned.1.call-done) | data formatting | bytes 8388608 | tf_op jit(solution)/shard_map/psum | solution.py:26
  188.5 4.4 gather_fusion.1
  193.2 1.1 select_select_fusion.1
  194.3 3.2 dynamic-slice_select_fusion
  197.6 146.0 %all-reduce.7.cloned.1.call-done = (f32[1024,512]{0,1:T(8,128)}, f32[512,512]{0,1:T(8,128)}) async-done(((f32[1024,512]{0,1:T(8,128)}, f32[512,512]{0,1:T(8,128)}), (f32[1024,512]{0,1:T(8,128)}, f32[512,512]{0,1:T(8,128)})) %all-reduce.7.cloned.1.call-update) | async-done | bytes 3145744 | tf_op jit(solution)/shard_map/psum | solution.py:9
  343.5 1.4 select_add_fusion
  345.6 11.7 %cholesky.102 = f32[128,128]{1,0:T(8,128)S(1)} custom-call(f32[128,128]{1,0:T(8,128)S(1)} %cholesky.260), custom_call_target="Cholesky" | custom-call | tf_op jit(solution)/shard_map/jit(cholesky)/cholesky | solution.py:33
  357.4 9.8 %custom-call.32 = f32[1,128,128]{1,2,0:T(8,128)S(1)} custom-call(f32[1,128,128]{2,1,0:T(8,128)S(1)} %get-tuple-element.38), custom_call_target="InvertDiagBlocksLowerTriangular" | custom-call | tf_op jit(solution)/shard_map/jit(cholesky)/cholesky | solution.py:33
  368.1 11.7 %cholesky.213 = f32[128,128]{1,0:T(8,128)S(1)} custom-call(f32[128,128]{1,0:T(8,128)S(1)} %cholesky.264), custom_call_target="Cholesky" | custom-call | tf_op jit(solution)/shard_map/jit(cholesky)/cholesky | solution.py:33
  379.9 10.1 %custom-call.33 = f32[1,128,128]{1,2,0:T(8,128)S(1)} custom-call(f32[1,128,128]{2,1,0:T(8,128)S(1)} %get-tuple-element.36), custom_call_target="InvertDiagBlocksLowerTriangular" | custom-call | tf_op jit(solution)/shard_map/jit(cholesky)/cholesky | solution.py:33
  390.6 1.5 convolution_subtract_fusion.5
  392.1 11.7 %cholesky.234 = f32[128,128]{1,0:T(8,128)S(1)} custom-call(f32[128,128]{1,0:T(8,128)S(1)} %cholesky.269), custom_call_target="Cholesky" | custom-call | tf_op jit(solution)/shard_map/jit(cholesky)/cholesky | solution.py:33
  403.9 9.8 %custom-call.34 = f32[1,128,128]{1,2,0:T(8,128)S(1)} custom-call(f32[1,128,128]{2,1,0:T(8,128)S(1)} %get-tuple-element.34), custom_call_target="InvertDiagBlocksLowerTriangular" | custom-call | tf_op jit(solution)/shard_map/jit(cholesky)/cholesky | solution.py:33
  414.0 1.3 convolution_subtract_fusion.6
  415.4 11.9 %cholesky.251 = f32[128,128]{1,0:T(8,128)S(1)} custom-call(f32[128,128]{1,0:T(8,128)S(1)} %convolution_subtract_fusion.6), custom_call_target="Cholesky" | custom-call | tf_op jit(solution)/shard_map/jit(cholesky)/cholesky | solution.py:33
  427.4 0.6 compare_reduce_fusion.1
  428.0 0.7 compare_reduce_fusion
  428.7 0.7 compare_reduce_fusion.2
  432.0 8.2 %while.1 = (s32[]{:T(128)}, f32[512,512]{0,1:T(8,128)S(1)}, s32[4,2]{0,1:T(2,128)S(1)}, f32[4,128,128]{2,1,0:T(8,128)S(1)}, s32[]{:T(128)}) while((s32[]{:T(128)}, f32[512,512]{0,1:T(8,128)S(1)}, s32[4,2]{0,1:T(2,128)S(1)}, f32[4,128,128]{2,1,0:T(8,128)S(1)}, s32[]{:T(128)}) %tuple.31), condition=%wide.while_cond, body=%wide.while_body.sunk | while | flops 2 | bytes 393329 | solution.py:35
  432.1 0.5 fusion.80
  432.6 1.3 dynamic-slice.7
  434.2 0.5 fusion.80
  434.7 1.3 dynamic-slice.7
  436.2 0.5 fusion.80
  436.7 1.3 dynamic-slice.7
  438.3 0.5 fusion.80
  438.8 1.3 dynamic-slice.7
  440.2 39.3 %custom-call.35 = f32[4,128,128]{1,2,0:T(8,128)S(1)} custom-call(f32[4,128,128]{2,1,0:T(8,128)S(1)} %get-tuple-element.12), custom_call_target="InvertDiagBlocksLowerTriangular" | custom-call | tf_op jit(solution)/shard_map/triangular_solve | solution.py:35
  479.5 2.4 fusion.35
  482.0 2.3 convolution_subtract_fusion.3
  484.2 1.1 fusion.57
  485.3 1.3 convolution_subtract_fusion.1
  486.6 1.1 fusion.59
  487.7 2.1 fusion.26
  489.7 1.1 fusion.61
  490.8 1.0 fusion.60
  491.8 1.0 convolution_subtract_fusion.2
  492.9 1.0 fusion.58
  493.9 1.5 convolution_subtract_fusion
  495.4 1.0 fusion.56
  496.4 2.0 fusion.23
  498.5 1.0 fusion.55
  499.5 16.5 %fusion.8 = f32[2048,1024]{1,0:T(8,128)} fusion(f32[2048,1024]{1,0:T(8,128)S(1)} %bitcast.60, f32[1024,512]{0,1:T(8,128)S(1)} %copy-done.3, f32[128,2048]{1,0:T(8,128)S(1)} %fusion.60, f32[128,2048]{1,0:T(8,128)S(1)} %fusion.58, f32[128,2048]{1,0:T(8,128)S(1)} %fusion.56, f32[128,2048]{1,0:T(8,128)S(1)} %fusion.55), kind=kOutput, calls=%fused_computation.13 | convolution fusion | flops 12890144768 | bytes 23068672 | tf_op jit(solution)/shard_map/dot_general | solution.py:38
  (61 shorter events, 3.9 us)
Async XLA Ops:
  6.5 176.6 %all-reduce.5.cloned.1.call-start = ((), (), s32[]{:S(2)}) async-start(), calls=%async_computation | async-start | bytes 8388608 | tf_op jit(solution)/shard_map/psum | solution.py:26
  29.8 313.7 %all-reduce.7.cloned.1.call-start = ((), (), s32[]{:S(2)}) async-start(), calls=%async_computation.1 | async-start | bytes 6291456 | tf_op jit(solution)/shard_map/psum | solution.py:9
  194.3 149.2 %copy-start.4 = (f32[512]{0:T(512)S(1)}, f32[512]{0:T(512)}, u32[]{:S(2)}) copy-start(f32[512]{0:T(512)} %param.5) | copy-start | bytes 6148
  343.5 1.8 copy-start.1
  345.6 34.4 %copy-start.2 = (f32[512,512]{1,0:T(8,128)}, f32[512,512]{1,0:T(8,128)S(1)}, u32[]{:S(2)}) copy-start(f32[512,512]{1,0:T(8,128)S(1)} %fusion.37) | copy-start | bytes 3145732
  479.5 5.8 %copy-start = (f32[2048,512]{0,1:T(8,128)S(1)}, f32[2048,512]{0,1:T(8,128)}, u32[]{:S(2)}) copy-start(f32[2048,512]{0,1:T(8,128)} %all-reduce.5.cloned.1.call-done) | copy-start | bytes 12582916
  492.9 6.6 %slice-start = ((s8[8388608]{0:T(1024)(128)(4,1)}), s8[4194304]{0:T(1024)(128)(4,1)S(1)}, s32[]{:S(2)}) async-start(s8[8388608]{0:T(1024)(128)(4,1)} %bitcast.59), calls=%async_computation.2 | async-start | bytes 8388608
  495.4 4.1 slice-start.1
  496.4 3.1 copy-start.3
Sparse Core Ops, SparseCore 0:
  30.0 153.1 all-reduce.4
  197.7 145.8 all-reduce.6
where the time goes:
time: 527 us; the launch traced here: 523 us
  waiting for transfers between devices  299 us (57%)
  other arithmetic  130 us (25%)
  matrix products  40.3 us (8%)
  local copies, waits for them, and re-layouts  37 us (7%)
  between operations  16.6 us (3%)
    psum x1, waiting for transfers between devices, local(): row_panel = lax.psum(partial_panel, 'col')  153 us
    psum x1, waiting for transfers between devices, spread(): return lax.psum(kept, axis)  146 us
    another operation x14, other arithmetic, local(): factor = jnp.linalg.cholesky(innovation)  78.9 us
    another operation x3, other arithmetic, local(): lax.linalg.triangular_solve(factor, forward, left_side=True, lower=True,...  39.4 us
    dot_general x1, matrix products, local(): lax.dot_general(col_panel, weighted, (((1,), (0,)), ((), ())), precision=...  16.5 us
    another operation x7, matrix products, local(): lax.linalg.triangular_solve(factor, row_panel.T, left_side=True, lower=True)  11.2 us
  transfers between devices with their start and end apart: 2, of which 2 were waited for; matrix products, arithmetic and copies ran while one was open for 0% of the time, Pallas kernels for 0%

commit v1 on v0

--- a/solution.py
+++ b/solution.py
@@ -1,7 +1,18 @@
+import functools
+
 import jax
 import jax.numpy as jnp
 from jax import lax
+from jax.experimental import pallas as pl
+from jax.experimental.pallas import tpu as pltpu
 from jax.sharding import PartitionSpec as P
+
+CAP = 96
+NB = 8
+K = CAP * NB
+BLK = 2048
+HI = lax.Precision.HIGHEST
+VM = 48 * 1024 * 1024
 
 
 def spread(value, axis, source):
@@ -9,7 +20,7 @@
     return lax.psum(kept, axis)
 
 
-def local(prior, observed, obs_noise):
+def general(prior, observed, obs_noise):
     rows_dev = prior.shape[0]
     cols_dev = prior.shape[1]
     row_id = lax.axis_index("row")
@@ -39,10 +50,311 @@
         col_panel,
         weighted,
         (((1,), (0,)), ((), ())),
-        precision=lax.Precision.HIGHEST,
+        precision=HI,
         preferred_element_type=jnp.float32,
     )
     return prior - update.T
+
+
+def split3(x):
+    hi = x.astype(jnp.bfloat16)
+    r = x - hi.astype(jnp.float32)
+    mid = r.astype(jnp.bfloat16)
+    lo = (r - mid.astype(jnp.float32)).astype(jnp.bfloat16)
+    return hi, mid, lo
+
+
+def split2(x):
+    hi = x.astype(jnp.bfloat16)
+    return hi, (x - hi.astype(jnp.float32)).astype(jnp.bfloat16)
+
+
+def dot(a, b, dims):
+    return lax.dot_general(a, b, (dims, ((), ())), preferred_element_type=jnp.float32)
+
+
+def rows_kernel(rows_ref, rowv_ref, col_ref, prior_ref, h_ref, s_ref, buf, sem):
+    def start(j, _):
+        r = jnp.clip(rows_ref[j], 0, BLK - 1)
+        pltpu.make_async_copy(prior_ref.at[pl.ds(r, 1)], buf.at[pl.ds(j, 1)], sem).start()
+        return 0
+
+    lax.fori_loop(0, CAP, start, 0, unroll=8)
+    pltpu.make_async_copy(prior_ref.at[pl.ds(0, CAP)], buf, sem).wait()
+    h = jnp.where(rowv_ref[...] >= 0, buf[...], 0.0)
+    h_ref[...] = h
+    cols = h.shape[1]
+    pick = (lax.broadcasted_iota(jnp.int32, (cols, CAP), 0) == col_ref[...]).astype(jnp.bfloat16)
+    s = 0.0
+    for part in split3(h):
+        s = s + dot(part, pick, ((1,), (0,)))
+    s_ref[...] = s
+
+
+def take_rows(prior, row_idx, col_idx):
+    cols = prior.shape[1]
+    return pl.pallas_call(
+        rows_kernel,
+        grid_spec=pltpu.PrefetchScalarGridSpec(
+            num_scalar_prefetch=1,
+            grid=(1,),
+            in_specs=[
+                pl.BlockSpec((CAP, 1), lambda i, r: (0, 0)),
+                pl.BlockSpec((1, CAP), lambda i, r: (0, 0)),
+                pl.BlockSpec(memory_space=pl.ANY),
+            ],
+            out_specs=[
+                pl.BlockSpec((CAP, cols), lambda i, r: (0, 0)),
+                pl.BlockSpec((CAP, CAP), lambda i, r: (0, 0)),
+            ],
+            scratch_shapes=[pltpu.VMEM((CAP, cols), jnp.float32), pltpu.SemaphoreType.DMA],
+        ),
+        out_shape=[
+            jax.ShapeDtypeStruct((CAP, cols), jnp.float32),
+            jax.ShapeDtypeStruct((CAP, CAP), jnp.float32),
+        ],
+        name="take_rows",
+    )(row_idx, row_idx[:, None], col_idx[None, :], prior)
+
+
+def cols_kernel(col_ref, prior_ref, g_ref):
+    cols = prior_ref.shape[1]
+    pick = (lax.broadcasted_iota(jnp.int32, (CAP, cols), 1) == col_ref[...]).astype(jnp.bfloat16)
+    g = 0.0
+    for part in split3(prior_ref[...]):
+        g = g + dot(pick, part, ((1,), (1,)))
+    g_ref[...] = g
+
+
+def take_cols(prior, col_idx):
+    rows, cols = prior.shape
+    tile = 256
+    return pl.pallas_call(
+        cols_kernel,
+        grid=(rows // tile,),
+        in_specs=[
+            pl.BlockSpec((CAP, 1), lambda i: (0, 0)),
+            pl.BlockSpec((tile, cols), lambda i: (i, 0)),
+        ],
+        out_specs=pl.BlockSpec((CAP, tile), lambda i: (0, i)),
+        out_shape=jax.ShapeDtypeStruct((CAP, rows), jnp.float32),
+        cost_estimate=pl.CostEstimate(flops=2 * CAP * rows * cols * 3, bytes_accessed=rows * cols * 4, transcendentals=0),
+        compiler_params=pltpu.CompilerParams(vmem_limit_bytes=VM),
+        name="take_cols",
+    )(col_idx[:, None], prior)
+
+
+def invert_kernel(count_ref, noise_ref, s_ref, out_ref, a_ref, d_ref):
+    eye = (
+        lax.broadcasted_iota(jnp.int32, (K, K), 0) == lax.broadcasted_iota(jnp.int32, (K, K), 1)
+    )
+    a_ref[...] = s_ref[...] + jnp.where(eye, noise_ref[...], 0.0)
+    lane8 = lax.broadcasted_iota(jnp.int32, (8, 128), 1)
+    sub8 = lax.broadcasted_iota(jnp.int32, (8, 128), 0)
+    eye8 = (lane8 == sub8).astype(jnp.float32)
+
+    def group(g, _):
+        at = pl.multiple_of(g * 8, 8)
+        r = d_ref[pl.ds(at, 8), :]
+        cols = [jnp.broadcast_to(r[:, k : k + 1], (8, 128)) for k in range(8)]
+        x = r - eye8
+        for k in range(8):
+            ck = cols[k]
+            inv = 1.0 / jnp.broadcast_to(ck[k : k + 1], (8, 128))
+            on = sub8 == k
+            f = jnp.where(on, 1.0 - inv, ck * inv)
+            x = x - f * jnp.broadcast_to(x[k : k + 1], (8, 128))
+            for j in range(k + 1, 8):
+                cols[j] = cols[j] - f * jnp.broadcast_to(cols[j][k : k + 1], (8, 128))
+        a = d_ref[...]
+        upd = a
+        for k in range(8):
+            upd = upd - jnp.broadcast_to(a[:, k : k + 1], a.shape) * jnp.broadcast_to(x[k : k + 1], a.shape)
+        d_ref[...] = pltpu.roll(upd, 120, 1)
+        d_ref[pl.ds(at, 8), :] = pltpu.roll(x - eye8, 120, 1)
+        return 0
+
+    lane_r = lax.broadcasted_iota(jnp.int32, (CAP, K), 1)
+    sub_r = lax.broadcasted_iota(jnp.int32, (CAP, K), 0)
+    for b in range(NB):
+        rows = pl.ds(b * CAP, CAP)
+        r = a_ref[rows, :]
+        d_ref[...] = jnp.where(
+            lax.broadcasted_iota(jnp.int32, (CAP, 128), 1) < CAP,
+            pltpu.roll(r, (K - b * CAP) % K, 1)[:, :128],
+            0.0,
+        )
+        groups = (count_ref[b] + 7) // 8
+        lax.fori_loop(0, groups, group, 0)
+        back = pltpu.roll(d_ref[...], groups * 8, 1)
+        sub_d = lax.broadcasted_iota(jnp.int32, (CAP, 128), 0)
+        lane_d = lax.broadcasted_iota(jnp.int32, (CAP, 128), 1)
+        inside = (sub_d < groups * 8) & (lane_d < groups * 8)
+        unit = (sub_d == lane_d).astype(jnp.float32)
+        dinv = jnp.where(inside, -back, unit)[:, :CAP]
+        eye_b = (lane_r == sub_r + b * CAP).astype(jnp.float32)
+        rp = r - eye_b
+        t = lax.dot_general(dinv, rp, (((1,), (0,)), ((), ())), precision=HI, preferred_element_type=jnp.float32)
+        a_ref[...] = a_ref[...] - lax.dot_general(
+            rp, t, (((0,), (0,)), ((), ())), precision=HI, preferred_element_type=jnp.float32
+        )
+        a_ref[rows, :] = t - eye_b
+    out_ref[...] = -a_ref[...]
+
+
+def invert(count, noise, s):
+    return pl.pallas_call(
+        invert_kernel,
+        grid_spec=pltpu.PrefetchScalarGridSpec(
+            num_scalar_prefetch=1,
+            grid=(1,),
+            in_specs=[
+                pl.BlockSpec((1, K), lambda i, c: (0, 0)),
+                pl.BlockSpec((K, K), lambda i, c: (0, 0)),
+            ],
+            out_specs=pl.BlockSpec((K, K), lambda i, c: (0, 0)),
+            scratch_shapes=[pltpu.VMEM((K, K), jnp.float32), pltpu.VMEM((CAP, 128), jnp.float32)],
+        ),
+        out_shape=jax.ShapeDtypeStruct((K, K), jnp.float32),
+        compiler_params=pltpu.CompilerParams(vmem_limit_bytes=VM),
+        name="invert",
+    )(count, noise[None, :], s)
+
+
+def final_kernel(core_ref, inv_ref, pc_ref, own_ref, other_ref, prior_ref, out_ref, wh_ref, wl_ref):
+    i = pl.program_id(0)
+
+    @pl.when(i == 0)
+    def _():
+        ih, il = split2(inv_ref[...])
+        ph, pll = split2(pc_ref[...])
+        w = dot(ih, ph, ((1,), (0,))) + (dot(ih, pll, ((1,), (0,))) + dot(il, ph, ((1,), (0,))))
+        wh, wl = split2(w)
+        wh_ref[...] = wh
+        wl_ref[...] = wl
+
+    def update(ref):
+        gh, gl = split2(ref[...])
+        d = ((0,), (0,))
+        u = dot(gh, wh_ref[...], d) + (dot(gh, wl_ref[...], d) + dot(gl, wh_ref[...], d))
+        out_ref[...] = prior_ref[...] - u
+
+    half = pl.num_programs(0) // 2
+
+    @pl.when(i < half)
+    def _():
+        update(own_ref)
+
+    @pl.when(i >= half)
+    def _():
+        update(other_ref)
+
+
+def final(core, inv, panel_c, own, other, prior):
+    rows, cols = prior.shape
+    tile = 256
+    n = rows // tile
+    half = n // 2
+
+    def place(i, c):
+        mine = i < half
+        return (jnp.where(mine, c[0] * half + i, (1 - c[0]) * half + i - half), 0)
+
+    return pl.pallas_call(
+        final_kernel,
+        grid_spec=pltpu.PrefetchScalarGridSpec(
+            num_scalar_prefetch=1,
+            grid=(n,),
+            in_specs=[
+                pl.BlockSpec((K, K), lambda i, c: (0, 0)),
+                pl.BlockSpec((K, cols), lambda i, c: (0, 0)),
+                pl.BlockSpec((K, tile), lambda i, c: (0, jnp.minimum(i, half - 1))),
+                pl.BlockSpec((K, tile), lambda i, c: (0, jnp.maximum(i - half, 0))),
+                pl.BlockSpec((tile, cols), place),
+            ],
+            out_specs=pl.BlockSpec((tile, cols), place),
+            scratch_shapes=[pltpu.VMEM((K, cols), jnp.bfloat16), pltpu.VMEM((K, cols), jnp.bfloat16)],
+        ),
+        out_shape=jax.ShapeDtypeStruct((rows, cols), jnp.float32),
+        compiler_params=pltpu.CompilerParams(vmem_limit_bytes=VM),
+        name="final",
+    )(core, inv, panel_c, own, other, prior)
+
+
+SWAP = [(i, i ^ 1) for i in range(16)]
+
+
+def swap_core(x):
+    return lax.ppermute(x, "col", SWAP)
+
+
+def all_blocks(x, axis):
+    if axis == "row":
+        perms = [[(i, i ^ d) for i in range(8)] for d in range(1, 8)]
+    else:
+        perms = [[(i, i ^ (2 * d)) for i in range(16)] for d in range(1, 8)]
+    return [x] + [lax.ppermute(x, axis, p) for p in perms]
+
+
+def in_order(pieces, me, axis):
+    bits = [(me >> k) & 1 for k in range(3)]
+    for k in range(3):
+        step = 1 << k
+        pieces = [
+            jnp.where(bits[k] == 1, pieces[d ^ step], pieces[d]) for d in range(8)
+        ]
+    return jnp.concatenate(pieces, axis=axis)
+
+
+def fast(prior, slot_state, slot_noise, count):
+    cols = prior.shape[1]
+    row_id = lax.axis_index("row")
+    col_id = lax.axis_index("col")
+    core = col_id % 2
+    chip_col = col_id // 2
+    state_r = lax.dynamic_slice_in_dim(slot_state, row_id * CAP, CAP)
+    state_c = lax.dynamic_slice_in_dim(slot_state, chip_col * CAP, CAP)
+    row_idx = jnp.where(state_r >= 0, state_r - row_id * BLK, -1)
+    col_idx = jnp.where(state_c >= 0, state_c - col_id * cols, -1)
+    h, s_part = take_rows(prior, row_idx, col_idx)
+    s_blk = s_part + swap_core(s_part)
+    s_rows = in_order(all_blocks(s_blk, "col"), chip_col, 1)
+    half = K // 2
+    s_half = jnp.where(core == 0, s_rows[:, :half], s_rows[:, half:])
+    s_cols = in_order(all_blocks(s_half, "row"), row_id, 0)
+    s_other = swap_core(s_cols)
+    s = jnp.concatenate(
+        [jnp.where(core == 0, s_cols, s_other), jnp.where(core == 0, s_other, s_cols)], axis=1
+    )
+    panel_c = in_order(all_blocks(h, "row"), row_id, 0)
+    g = take_cols(prior, col_idx)
+    hr = BLK // 2
+    keep = jnp.where(core == 0, g[:, :hr], g[:, hr:])
+    give = jnp.where(core == 0, g[:, hr:], g[:, :hr])
+    own = in_order(all_blocks(keep + swap_core(give), "col"), chip_col, 0)
+    other = swap_core(own)
+    inv = invert(count, slot_noise, s)
+    return final(core.astype(jnp.int32)[None], inv, panel_c, own, other, prior)
+
+
+def local(prior, observed, obs_noise):
+    block = observed // BLK
+    m = observed.shape[0]
+    earlier = lax.broadcasted_iota(jnp.int32, (m, m), 1) < lax.broadcasted_iota(jnp.int32, (m, m), 0)
+    same = block[:, None] == block[None, :]
+    rank = jnp.sum((same & earlier).astype(jnp.int32), axis=1)
+    count = jnp.sum((block[None, :] == jnp.arange(NB)[:, None]).astype(jnp.int32), axis=1)
+    fits = jnp.max(count) <= CAP
+    slot = block * CAP + rank
+    hit = slot[None, :] == jnp.arange(K)[:, None]
+    slot_state = jnp.sum(jnp.where(hit, observed[None, :] + 1, 0), axis=1) - 1
+    slot_noise = jnp.sum(jnp.where(hit, obs_noise[None, :], 0.0), axis=1)
+    slot_noise = jnp.where(slot_state >= 0, slot_noise, 1.0)
+    return lax.cond(
+        fits,
+        lambda: fast(prior, slot_state, slot_noise, count),
+        lambda: general(prior, observed, obs_noise),
+    )
 
 
 def solution(mesh):

time: 527 us -> 232 us (0.44)
  waiting for transfers between devices: 299 us -> 45.6 us
  other arithmetic: 130 us -> 16.7 us
  Pallas kernels: 0 us -> 77.5 us
  starting transfers between devices: 0.04 us -> 62.4 us
  matrix products: 40.3 us -> 0 us
  local copies, waits for them, and re-layouts: 37 us -> 0.96 us
  loops' own time: 0.14 us -> 9.55 us
    psum x2 -> x0, waiting for transfers between devices: 299 us -> none  [the longest x1 153 us: local(): row_panel = lax.psum(partial_panel, 'col')]
    another operation x17 -> x0, other arithmetic: 118 us -> none  [the longest x14 78.9 us: local(): factor = jnp.linalg.cholesky(innovation)]
    pallas_call x0 -> x4, Pallas kernels: none -> 77.5 us  [the longest x1 46.3 us: invert(): pl.pallas_call(invert_kernel, grid_spec=pltpu.PrefetchScalarGridSpec(num_...]
    ppermute x0 -> x32, starting transfers between devices: none -> 62.4 us  [the longest x28 48.9 us: all_blocks(): return [x] + [lax.ppermute(x, axis, p) for p in perms]]
    ppermute x0 -> x32, waiting for transfers between devices: none -> 45.6 us  [the longest x28 44.5 us: all_blocks(): return [x] + [lax.ppermute(x, axis, p) for p in perms]]
    another operation x20 -> x0, matrix products: 23.8 us -> none  [the longest x7 11.2 us: local(): lax.linalg.triangular_solve(factor, row_panel.T, left_side=True, lower=True)]
    dot_general x1 -> x0, matrix products: 16.5 us -> none  [local(): lax.dot_general(col_panel, weighted, (((1,), (0,)), ((), ())), precision=...]
    gather x3 -> x0, local copies, waits for them, and re-layouts: 13.5 us -> none  [the longest x1 8.76 us: local(): jnp.take(prior, col_pick, axis=1)]
  transfers between devices with their start and end apart: 2 -> 32, of which waited for: 2 -> 16; matrix products, arithmetic and copies ran while one was open for 0% -> 4% of each run, Pallas kernels for 0% -> 24%
where the time goes in v1:
time: 232 us; the launch traced here: 227 us
  Pallas kernels  77.5 us (33%)
  starting transfers between devices  62.4 us (27%)
  waiting for transfers between devices  45.6 us (20%)
  other arithmetic  16.7 us (7%)
  between operations  14.3 us (6%)
  loops' own time  9.55 us (4%)
    ppermute x28, starting transfers between devices, all_blocks(): return [x] + [lax.ppermute(x, axis, p) for p in perms]  48.9 us
    pallas_call x1, Pallas kernels, invert(): pl.pallas_call(invert_kernel, grid_spec=pltpu.PrefetchScalarGridSpec(num_...  46.3 us
    ppermute x28, waiting for transfers between devices, all_blocks(): return [x] + [lax.ppermute(x, axis, p) for p in perms]  44.5 us
    pallas_call x1, Pallas kernels, final(): pl.pallas_call(final_kernel, grid_spec=pltpu.PrefetchScalarGridSpec(num_s...  18.2 us
    ppermute x4, starting transfers between devices, swap_core(): return lax.ppermute(x, 'col', SWAP)  13.5 us
    another operation x1, loops' own time, local(): lax.cond(fits, lambda: fast(prior, slot_state, slot_noise, count), lambda...  9.55 us
    pallas_call x1, Pallas kernels, take_cols(): pl.pallas_call(cols_kernel, grid=(rows // tile,), in_specs=[pl.BlockSpec(...  8.37 us
    cond x22, other arithmetic  8.19 us
  transfers between devices with their start and end apart: 32, of which 16 were waited for; matrix products, arithmetic and copies ran while one was open for 4% of the time, Pallas kernels for 24%

profile of v1, /device:TPU:1, one launch (start us, length us, event | category | flops | bytes accessed | tf_op | source)
XLA Modules:
  0.0 227.0 jit_solution(16289949641512423957)
XLA Ops:
  7.3 1.1 fusion.68
  9.9 210.0 %conditional.1 = (f32[2048,1024]{1,0:T(8,128)}) conditional(s32[]{:T(128)} %convert_element_type.12, (s32[512]{0:T(512)}, f32[2048,1024]{1,0:T(8,128)}, f32[512]{0:T(512)}) %tuple.30, (s32[512]{0:T(512)S(1)}, s32[512,512]{1,0:T(8,128)}, s32[768,512]{1,0:T(8,128)S(1)}, s32[512]{0:T(512)}, f32[512]{0:T(512)}, /*index=5*/f32[2048,1024]{1,0:T(8,128)}, ...), branch_computations={%region_2.14_spmd, %region_14.18_spmd} | conditional | flops 21360162816 | bytes 237677376 | solution.py:353
  18.9 1.4 reduce_sum.35
  22.0 0.7 copy.20.rowv_ref
  22.8 4.6 %take_rows.1 = (f32[96,1024]{1,0:T(8,128)}, f32[96,96]{1,0:T(8,128)}) custom-call(s32[96]{0:T(128)} %copy-done.8, s32[96,1]{1,0:T(8,128)} %copy.20.rowv_ref, s32[1,96]{1,0:T(1,128)} %bitcast.71, f32[2048,1024]{1,0:T(8,128)} %get-tuple-element.71.prior_ref), custom_call_target="tpu_custom_call" | custom-call | tf_op jit(solution)/shard_map/cond/branch_1_fun/take_rows/pallas_call | solution.py:96
  27.4 1.5 collective-permute-start
  28.9 1.1 collective-permute-done
  30.0 0.8 add.102
  30.8 5.3 %collective-permute-start.1 = (f32[96,96]{1,0:T(8,128)S(1)}, f32[96,96]{1,0:T(8,128)S(1)}, u32[]{:S(2)}, u32[]{:S(2)}) collective-permute-start(f32[96,96]{1,0:T(8,128)S(1)} %add.102), channel_id=1, source_target_pairs={{0,14},{1,15},{2,12},{3,13},{4,10},{5,11},{6,8},{7,9},{8,6},{9,7},... | collective-permute-start | bytes 110600 | tf_op jit(solution)/shard_map/cond/branch_1_fun/ppermute | solution.py:296
  36.4 2.6 %collective-permute-start.3 = (f32[96,96]{1,0:T(8,128)S(1)}, f32[96,96]{1,0:T(8,128)S(1)}, u32[]{:S(2)}, u32[]{:S(2)}) collective-permute-start(f32[96,96]{1,0:T(8,128)S(1)} %add.102), channel_id=1, source_target_pairs={{0,10},{1,11},{2,8},{3,9},{4,14},{5,15},{6,12},{7,13},{8,2},{9,3},... | collective-permute-start | bytes 110600 | tf_op jit(solution)/shard_map/cond/branch_1_fun/ppermute | solution.py:296
  39.4 2.5 %collective-permute-start.5 = (f32[96,96]{1,0:T(8,128)S(1)}, f32[96,96]{1,0:T(8,128)S(1)}, u32[]{:S(2)}, u32[]{:S(2)}) collective-permute-start(f32[96,96]{1,0:T(8,128)S(1)} %add.102), channel_id=1, source_target_pairs={{0,6},{1,7},{2,4},{3,5},{4,2},{5,3},{6,0},{7,1},{8,14},{9,15},{10,... | collective-permute-start | bytes 110600 | tf_op jit(solution)/shard_map/cond/branch_1_fun/ppermute | solution.py:296
  43.9 2.5 %collective-permute-done.6 = f32[96,96]{1,0:T(8,128)S(1)} collective-permute-done((f32[96,96]{1,0:T(8,128)S(1)}, f32[96,96]{1,0:T(8,128)S(1)}, u32[]{:S(2)}, u32[]{:S(2)}) %collective-permute-start.6) | collective-permute-done | bytes 36896 | tf_op jit(solution)/shard_map/cond/branch_1_fun/ppermute | solution.py:296
  46.7 4.5 %collective-permute-start.10 = (f32[96,384]{1,0:T(8,128)S(1)}, f32[96,384]{1,0:T(8,128)S(1)}, u32[]{:S(2)}, u32[]{:S(2)}) collective-permute-start(f32[96,384]{1,0:T(8,128)S(1)} %maximum_select_fusion), channel_id=1, source_target_pairs={{0,80},{16,64},{32,112},{48,96},{64,16},{80,0},{96,48},{112,32},{1... | collective-permute-start | bytes 442376 | tf_op jit(solution)/shard_map/cond/branch_1_fun/ppermute | solution.py:296
  51.3 8.4 %take_cols.1 = f32[96,2048]{1,0:T(8,128)S(1)} custom-call(s32[96,1]{1,0:T(8,128)S(1)} %copy.21.col_ref, f32[2048,1024]{1,0:T(8,128)} %get-tuple-element.71.prior_ref), custom_call_target="tpu_custom_call" | custom-call | flops 1207959552 | bytes 8388608 | tf_op jit(solution)/shard_map/cond/branch_1_fun/take_cols/pallas_call | solution.py:132
  59.7 1.5 collective-permute-start.12
  62.4 3.7 %collective-permute-start.8 = (f32[96,384]{1,0:T(8,128)S(1)}, f32[96,384]{1,0:T(8,128)S(1)}, u32[]{:S(2)}, u32[]{:S(2)}) collective-permute-start(f32[96,384]{1,0:T(8,128)S(1)} %maximum_select_fusion), channel_id=1, source_target_pairs={{0,112},{16,96},{32,80},{48,64},{64,48},{80,32},{96,16},{112,0},{1... | collective-permute-start | bytes 442376 | tf_op jit(solution)/shard_map/cond/branch_1_fun/ppermute | solution.py:296
  66.2 4.7 %collective-permute-start.23 = (f32[96,1024]{1,0:T(8,128)S(1)}, f32[96,1024]{1,0:T(8,128)S(1)}, u32[]{:S(2)}, u32[]{:S(2)}) collective-permute-start(f32[96,1024]{1,0:T(8,128)S(1)} %slice_select_fusion), channel_id=1, source_target_pairs={{0,1},{1,0},{2,3},{3,2},{4,5},{5,4},{6,7},{7,6},{8,9},{9,8},{10,11... | collective-permute-start | bytes 1179656 | tf_op jit(solution)/shard_map/cond/branch_1_fun/ppermute | solution.py:288
  70.9 0.8 collective-permute-done.8
  72.6 3.4 %collective-permute-start.24 = (f32[96,1024]{1,0:T(8,128)S(1)}, f32[96,1024]{1,0:T(8,128)S(1)}, u32[]{:S(2)}, u32[]{:S(2)}) collective-permute-start(f32[96,1024]{1,0:T(8,128)S(1)} %select_add_fusion), channel_id=1, source_target_pairs={{0,14},{1,15},{2,12},{3,13},{4,10},{5,11},{6,8},{7,9},{8,6},{9,7},... | collective-permute-start | bytes 1179656 | tf_op jit(solution)/shard_map/cond/branch_1_fun/ppermute | solution.py:296
  76.0 1.2 collective-permute-start.25
  77.2 3.9 %collective-permute-start.26 = (f32[96,1024]{1,0:T(8,128)S(1)}, f32[96,1024]{1,0:T(8,128)S(1)}, u32[]{:S(2)}, u32[]{:S(2)}) collective-permute-start(f32[96,1024]{1,0:T(8,128)S(1)} %select_add_fusion), channel_id=1, source_target_pairs={{0,10},{1,11},{2,8},{3,9},{4,14},{5,15},{6,12},{7,13},{8,2},{9,3},... | collective-permute-start | bytes 1179656 | tf_op jit(solution)/shard_map/cond/branch_1_fun/ppermute | solution.py:296
  81.2 1.1 collective-permute-start.28
  82.3 1.2 collective-permute-done.24
  83.5 7.0 %collective-permute-done.25 = f32[96,1024]{1,0:T(8,128)S(1)} collective-permute-done((f32[96,1024]{1,0:T(8,128)S(1)}, f32[96,1024]{1,0:T(8,128)S(1)}, u32[]{:S(2)}, u32[]{:S(2)}) %collective-permute-start.25) | collective-permute-done | bytes 393248 | tf_op jit(solution)/shard_map/cond/branch_1_fun/ppermute | solution.py:296
  90.4 1.2 collective-permute-start.30
  91.7 6.4 %collective-permute-done.26 = f32[96,1024]{1,0:T(8,128)S(1)} collective-permute-done((f32[96,1024]{1,0:T(8,128)S(1)}, f32[96,1024]{1,0:T(8,128)S(1)}, u32[]{:S(2)}, u32[]{:S(2)}) %collective-permute-start.26) | collective-permute-done | bytes 393248 | tf_op jit(solution)/shard_map/cond/branch_1_fun/ppermute | solution.py:296
  98.0 4.4 %collective-permute-start.16 = (f32[96,1024]{1,0:T(8,128)S(1)}, f32[96,1024]{1,0:T(8,128)S(1)}, u32[]{:S(2)}, u32[]{:S(2)}) collective-permute-start(f32[96,1024]{1,0:T(8,128)S(1)} %copy-done.4), channel_id=1, source_target_pairs={{0,112},{16,96},{32,80},{48,64},{64,48},{80,32},{96,16},{112,0},{1... | collective-permute-start | bytes 1179656 | tf_op jit(solution)/shard_map/cond/branch_1_fun/ppermute | solution.py:296
  102.5 3.5 %collective-permute-done.27 = f32[96,1024]{1,0:T(8,128)S(1)} collective-permute-done((f32[96,1024]{1,0:T(8,128)S(1)}, f32[96,1024]{1,0:T(8,128)S(1)}, u32[]{:S(2)}, u32[]{:S(2)}) %collective-permute-start.27) | collective-permute-done | bytes 393248 | tf_op jit(solution)/shard_map/cond/branch_1_fun/ppermute | solution.py:296
  106.0 4.4 %collective-permute-start.17 = (f32[96,1024]{1,0:T(8,128)S(1)}, f32[96,1024]{1,0:T(8,128)S(1)}, u32[]{:S(2)}, u32[]{:S(2)}) collective-permute-start(f32[96,1024]{1,0:T(8,128)S(1)} %copy-done.4), channel_id=1, source_target_pairs={{0,96},{16,112},{32,64},{48,80},{64,32},{80,48},{96,0},{112,16},{1... | collective-permute-start | bytes 1179656 | tf_op jit(solution)/shard_map/cond/branch_1_fun/ppermute | solution.py:296
  110.4 2.2 collective-permute-done.28
  112.6 3.3 %collective-permute-start.19 = (f32[96,1024]{1,0:T(8,128)S(1)}, f32[96,1024]{1,0:T(8,128)S(1)}, u32[]{:S(2)}, u32[]{:S(2)}) collective-permute-start(f32[96,1024]{1,0:T(8,128)S(1)} %copy-done.4), channel_id=1, source_target_pairs={{0,64},{16,80},{32,96},{48,112},{64,0},{80,16},{96,32},{112,48},{1... | collective-permute-start | bytes 1179656 | tf_op jit(solution)/shard_map/cond/branch_1_fun/ppermute | solution.py:296
  116.8 1.2 select_dynamic-update-slice_fusion.7
  118.0 1.2 select_dynamic-update-slice_fusion.6
  119.2 0.8 select_dynamic-update-slice_fusion.5
  120.0 0.8 select_dynamic-update-slice_fusion.4
  120.9 0.8 select_dynamic-update-slice_fusion.3
  121.7 0.8 select_dynamic-update-slice_fusion.2
  122.5 0.8 select_dynamic-update-slice_fusion.1
  123.4 0.9 select_dynamic-update-slice_fusion.own_ref
  124.2 1.3 collective-permute-start.21
  125.5 8.6 %collective-permute-done.17 = f32[96,1024]{1,0:T(8,128)S(1)} collective-permute-done((f32[96,1024]{1,0:T(8,128)S(1)}, f32[96,1024]{1,0:T(8,128)S(1)}, u32[]{:S(2)}, u32[]{:S(2)}) %collective-permute-start.17) | collective-permute-done | bytes 393248 | tf_op jit(solution)/shard_map/cond/branch_1_fun/ppermute | solution.py:296
  134.2 2.0 collective-permute-start.22
  136.1 3.9 %collective-permute-start.31 = (f32[768,1024]{1,0:T(8,128)}, f32[768,1024]{1,0:T(8,128)}, u32[]{:S(2)}, u32[]{:S(2)}) collective-permute-start(f32[768,1024]{1,0:T(8,128)} %select_dynamic-update-slice_fusion.own_ref), channel_id=1, source_target_pairs={{0,1},{1,0},{2,3},{3,2},{4,5},{5,4},{6,7},{7,6},{8,9},{9,8},{10,11... | collective-permute-start | bytes 9437192 | tf_op jit(solution)/shard_map/cond/branch_1_fun/ppermute | solution.py:288
  140.2 5.5 %collective-permute-done.19 = f32[96,1024]{1,0:T(8,128)S(1)} collective-permute-done((f32[96,1024]{1,0:T(8,128)S(1)}, f32[96,1024]{1,0:T(8,128)S(1)}, u32[]{:S(2)}, u32[]{:S(2)}) %collective-permute-start.19) | collective-permute-done | bytes 393248 | tf_op jit(solution)/shard_map/cond/branch_1_fun/ppermute | solution.py:296
  145.6 3.4 %collective-permute-start.15 = (f32[768,384]{1,0:T(8,128)S(1)}, f32[768,384]{1,0:T(8,128)S(1)}, u32[]{:S(2)}, u32[]{:S(2)}) collective-permute-start(f32[768,384]{1,0:T(8,128)S(1)} %select_dynamic-update-slice_fusion.16), channel_id=1, source_target_pairs={{0,1},{1,0},{2,3},{3,2},{4,5},{5,4},{6,7},{7,6},{8,9},{9,8},{10,11... | collective-permute-start | bytes 3538952 | tf_op jit(solution)/shard_map/cond/branch_1_fun/ppermute | solution.py:288
  149.0 4.3 %collective-permute-done.21 = f32[96,1024]{1,0:T(8,128)S(1)} collective-permute-done((f32[96,1024]{1,0:T(8,128)S(1)}, f32[96,1024]{1,0:T(8,128)S(1)}, u32[]{:S(2)}, u32[]{:S(2)}) %collective-permute-start.21) | collective-permute-done | bytes 393248 | tf_op jit(solution)/shard_map/cond/branch_1_fun/ppermute | solution.py:296
  155.2 46.3 %invert.1.inv_ref = f32[768,768]{1,0:T(8,128)S(1)} custom-call(s32[8]{0:T(128)S(1)} %get-tuple-element.65.count_ref, f32[1,768]{1,0:T(1,128)S(1)} %select_n.420.noise_ref, f32[768,768]{1,0:T(8,128)S(1)} %pad_maximum_fusion.s_ref), custom_call_target="tpu_custom_call" | custom-call | tf_op jit(solution)/shard_map/cond/branch_1_fun/invert/pallas_call | solution.py:206
  201.6 18.2 %final.1 = f32[2048,1024]{1,0:T(8,128)} custom-call(s32[1]{0:T(128)} %bitcast.13.core_ref, f32[768,768]{1,0:T(8,128)S(1)} %invert.1.inv_ref, f32[768,1024]{1,0:T(8,128)S(1)} %select_dynamic-update-slice_fusion.8.pc_ref, f32[768,1024]{1,0:T(8,128)} %select_dynamic-update-slice_fusion.own_ref, f32[768,1024]{1,0:T(8,128)} %collective-permute-done.31.other_ref, ...), custom_call_target="tpu_custom_call" | custom-call | tf_op jit(solution)/shard_map/cond/branch_1_fun/final/pallas_call | solution.py:263
  (82 shorter events, 11.4 us)
Async XLA Ops:
  22.0 0.7 copy-start.8
  22.7 20.2 %copy-start.6 = (f32[512]{0:T(512)S(1)}, f32[512]{0:T(512)}, u32[]{:S(2)}) copy-start(f32[512]{0:T(512)} %get-tuple-element.70) | copy-start | bytes 6148 | tf_op jit(solution)/shard_map/cond
  22.8 28.4 %copy-start.7 = (s32[96]{0:T(128)S(1)}, s32[96]{0:T(128)}, u32[]{:S(2)}) copy-start(s32[96]{0:T(128)} %get-tuple-element.162) | copy-start | bytes 1156 | tf_op jit(solution)/shard_map/cond
  27.4 2.6 %collective-permute-start = (f32[96,96]{1,0:T(8,128)}, f32[96,96]{1,0:T(8,128)S(1)}, u32[]{:S(2)}, u32[]{:S(2)}) collective-permute-start(f32[96,96]{1,0:T(8,128)} %get-tuple-element.72), channel_id=1, source_target_pairs={{0,1},{1,0},{2,3},{3,2},{4,5},{5,4},{6,7},{7,6},{8,9},{9,8},{10,11... | collective-permute-start | bytes 110600 | tf_op jit(solution)/shard_map/cond/branch_1_fun/ppermute | solution.py:288
  30.8 11.2 %collective-permute-start.1 = (f32[96,96]{1,0:T(8,128)S(1)}, f32[96,96]{1,0:T(8,128)S(1)}, u32[]{:S(2)}, u32[]{:S(2)}) collective-permute-start(f32[96,96]{1,0:T(8,128)S(1)} %add.102), channel_id=1, source_target_pairs={{0,14},{1,15},{2,12},{3,13},{4,10},{5,11},{6,8},{7,9},{8,6},{9,7},... | collective-permute-start | bytes 110600 | tf_op jit(solution)/shard_map/cond/branch_1_fun/ppermute | solution.py:296
  36.1 6.8 %collective-permute-start.2 = (f32[96,96]{1,0:T(8,128)S(1)}, f32[96,96]{1,0:T(8,128)S(1)}, u32[]{:S(2)}, u32[]{:S(2)}) collective-permute-start(f32[96,96]{1,0:T(8,128)S(1)} %add.102), channel_id=1, source_target_pairs={{0,12},{1,13},{2,14},{3,15},{4,8},{5,9},{6,10},{7,11},{8,4},{9,5},... | collective-permute-start | bytes 110600 | tf_op jit(solution)/shard_map/cond/branch_1_fun/ppermute | solution.py:296
  36.4 6.9 %collective-permute-start.3 = (f32[96,96]{1,0:T(8,128)S(1)}, f32[96,96]{1,0:T(8,128)S(1)}, u32[]{:S(2)}, u32[]{:S(2)}) collective-permute-start(f32[96,96]{1,0:T(8,128)S(1)} %add.102), channel_id=1, source_target_pairs={{0,10},{1,11},{2,8},{3,9},{4,14},{5,15},{6,12},{7,13},{8,2},{9,3},... | collective-permute-start | bytes 110600 | tf_op jit(solution)/shard_map/cond/branch_1_fun/ppermute | solution.py:296
  39.0 4.7 %collective-permute-start.4 = (f32[96,96]{1,0:T(8,128)S(1)}, f32[96,96]{1,0:T(8,128)S(1)}, u32[]{:S(2)}, u32[]{:S(2)}) collective-permute-start(f32[96,96]{1,0:T(8,128)S(1)} %add.102), channel_id=1, source_target_pairs={{0,8},{1,9},{2,10},{3,11},{4,12},{5,13},{6,14},{7,15},{8,0},{9,1},... | collective-permute-start | bytes 110600 | tf_op jit(solution)/shard_map/cond/branch_1_fun/ppermute | solution.py:296
  39.4 4.5 %collective-permute-start.5 = (f32[96,96]{1,0:T(8,128)S(1)}, f32[96,96]{1,0:T(8,128)S(1)}, u32[]{:S(2)}, u32[]{:S(2)}) collective-permute-start(f32[96,96]{1,0:T(8,128)S(1)} %add.102), channel_id=1, source_target_pairs={{0,6},{1,7},{2,4},{3,5},{4,2},{5,3},{6,0},{7,1},{8,14},{9,15},{10,... | collective-permute-start | bytes 110600 | tf_op jit(solution)/shard_map/cond/branch_1_fun/ppermute | solution.py:296
  41.9 4.4 %collective-permute-start.6 = (f32[96,96]{1,0:T(8,128)S(1)}, f32[96,96]{1,0:T(8,128)S(1)}, u32[]{:S(2)}, u32[]{:S(2)}) collective-permute-start(f32[96,96]{1,0:T(8,128)S(1)} %add.102), channel_id=1, source_target_pairs={{0,4},{1,5},{2,6},{3,7},{4,0},{5,1},{6,2},{7,3},{8,12},{9,13},{10,... | collective-permute-start | bytes 110600 | tf_op jit(solution)/shard_map/cond/branch_1_fun/ppermute | solution.py:296
  42.9 3.5 %collective-permute-start.7 = (f32[96,96]{1,0:T(8,128)S(1)}, f32[96,96]{1,0:T(8,128)S(1)}, u32[]{:S(2)}, u32[]{:S(2)}) collective-permute-start(f32[96,96]{1,0:T(8,128)S(1)} %add.102), channel_id=1, source_target_pairs={{0,2},{1,3},{2,0},{3,1},{4,6},{5,7},{6,4},{7,5},{8,10},{9,11},{10,... | collective-permute-start | bytes 110600 | tf_op jit(solution)/shard_map/cond/branch_1_fun/ppermute | solution.py:296
  46.7 15.7 %collective-permute-start.10 = (f32[96,384]{1,0:T(8,128)S(1)}, f32[96,384]{1,0:T(8,128)S(1)}, u32[]{:S(2)}, u32[]{:S(2)}) collective-permute-start(f32[96,384]{1,0:T(8,128)S(1)} %maximum_select_fusion), channel_id=1, source_target_pairs={{0,80},{16,64},{32,112},{48,96},{64,16},{80,0},{96,48},{112,32},{1... | collective-permute-start | bytes 442376 | tf_op jit(solution)/shard_map/cond/branch_1_fun/ppermute | solution.py:296
  51.2 15.0 %collective-permute-start.11 = (f32[96,384]{1,0:T(8,128)S(1)}, f32[96,384]{1,0:T(8,128)S(1)}, u32[]{:S(2)}, u32[]{:S(2)}) collective-permute-start(f32[96,384]{1,0:T(8,128)S(1)} %maximum_select_fusion), channel_id=1, source_target_pairs={{0,64},{16,80},{32,96},{48,112},{64,0},{80,16},{96,32},{112,48},{1... | collective-permute-start | bytes 442376 | tf_op jit(solution)/shard_map/cond/branch_1_fun/ppermute | solution.py:296
  59.7 6.5 %collective-permute-start.12 = (f32[96,384]{1,0:T(8,128)S(1)}, f32[96,384]{1,0:T(8,128)S(1)}, u32[]{:S(2)}, u32[]{:S(2)}) collective-permute-start(f32[96,384]{1,0:T(8,128)S(1)} %maximum_select_fusion), channel_id=1, source_target_pairs={{0,48},{16,32},{32,16},{48,0},{64,112},{80,96},{96,80},{112,64},{1... | collective-permute-start | bytes 442376 | tf_op jit(solution)/shard_map/cond/branch_1_fun/ppermute | solution.py:296
  61.2 9.7 %collective-permute-start.13 = (f32[96,384]{1,0:T(8,128)S(1)}, f32[96,384]{1,0:T(8,128)S(1)}, u32[]{:S(2)}, u32[]{:S(2)}) collective-permute-start(f32[96,384]{1,0:T(8,128)S(1)} %maximum_select_fusion), channel_id=1, source_target_pairs={{0,32},{16,48},{32,0},{48,16},{64,96},{80,112},{96,64},{112,80},{1... | collective-permute-start | bytes 442376 | tf_op jit(solution)/shard_map/cond/branch_1_fun/ppermute | solution.py:296
  61.8 9.1 %collective-permute-start.14 = (f32[96,384]{1,0:T(8,128)S(1)}, f32[96,384]{1,0:T(8,128)S(1)}, u32[]{:S(2)}, u32[]{:S(2)}) collective-permute-start(f32[96,384]{1,0:T(8,128)S(1)} %maximum_select_fusion), channel_id=1, source_target_pairs={{0,16},{16,0},{32,48},{48,32},{64,80},{80,64},{96,112},{112,96},{1... | collective-permute-start | bytes 442376 | tf_op jit(solution)/shard_map/cond/branch_1_fun/ppermute | solution.py:296
  62.4 9.2 %collective-permute-start.8 = (f32[96,384]{1,0:T(8,128)S(1)}, f32[96,384]{1,0:T(8,128)S(1)}, u32[]{:S(2)}, u32[]{:S(2)}) collective-permute-start(f32[96,384]{1,0:T(8,128)S(1)} %maximum_select_fusion), channel_id=1, source_target_pairs={{0,112},{16,96},{32,80},{48,64},{64,48},{80,32},{96,16},{112,0},{1... | collective-permute-start | bytes 442376 | tf_op jit(solution)/shard_map/cond/branch_1_fun/ppermute | solution.py:296
  66.2 6.1 %collective-permute-start.9 = (f32[96,384]{1,0:T(8,128)S(1)}, f32[96,384]{1,0:T(8,128)S(1)}, u32[]{:S(2)}, u32[]{:S(2)}) collective-permute-start(f32[96,384]{1,0:T(8,128)S(1)} %maximum_select_fusion), channel_id=1, source_target_pairs={{0,96},{16,112},{32,64},{48,80},{64,32},{80,48},{96,0},{112,16},{1... | collective-permute-start | bytes 442376 | tf_op jit(solution)/shard_map/cond/branch_1_fun/ppermute | solution.py:296
  66.2 6.3 %collective-permute-start.23 = (f32[96,1024]{1,0:T(8,128)S(1)}, f32[96,1024]{1,0:T(8,128)S(1)}, u32[]{:S(2)}, u32[]{:S(2)}) collective-permute-start(f32[96,1024]{1,0:T(8,128)S(1)} %slice_select_fusion), channel_id=1, source_target_pairs={{0,1},{1,0},{2,3},{3,2},{4,5},{5,4},{6,7},{7,6},{8,9},{9,8},{10,11... | collective-permute-start | bytes 1179656 | tf_op jit(solution)/shard_map/cond/branch_1_fun/ppermute | solution.py:288
  72.4 25.6 %copy-start.4 = (f32[96,1024]{1,0:T(8,128)S(1)}, f32[96,1024]{1,0:T(8,128)}, u32[]{:S(2)}) copy-start(f32[96,1024]{1,0:T(8,128)} %get-tuple-element.73) | copy-start | bytes 1179652 | tf_op jit(solution)/shard_map/cond
  72.6 10.9 %collective-permute-start.24 = (f32[96,1024]{1,0:T(8,128)S(1)}, f32[96,1024]{1,0:T(8,128)S(1)}, u32[]{:S(2)}, u32[]{:S(2)}) collective-permute-start(f32[96,1024]{1,0:T(8,128)S(1)} %select_add_fusion), channel_id=1, source_target_pairs={{0,14},{1,15},{2,12},{3,13},{4,10},{5,11},{6,8},{7,9},{8,6},{9,7},... | collective-permute-start | bytes 1179656 | tf_op jit(solution)/shard_map/cond/branch_1_fun/ppermute | solution.py:296
  76.0 14.5 %collective-permute-start.25 = (f32[96,1024]{1,0:T(8,128)S(1)}, f32[96,1024]{1,0:T(8,128)S(1)}, u32[]{:S(2)}, u32[]{:S(2)}) collective-permute-start(f32[96,1024]{1,0:T(8,128)S(1)} %select_add_fusion), channel_id=1, source_target_pairs={{0,12},{1,13},{2,14},{3,15},{4,8},{5,9},{6,10},{7,11},{8,4},{9,5},... | collective-permute-start | bytes 1179656 | tf_op jit(solution)/shard_map/cond/branch_1_fun/ppermute | solution.py:296
  77.2 20.8 %collective-permute-start.26 = (f32[96,1024]{1,0:T(8,128)S(1)}, f32[96,1024]{1,0:T(8,128)S(1)}, u32[]{:S(2)}, u32[]{:S(2)}) collective-permute-start(f32[96,1024]{1,0:T(8,128)S(1)} %select_add_fusion), channel_id=1, source_target_pairs={{0,10},{1,11},{2,8},{3,9},{4,14},{5,15},{6,12},{7,13},{8,2},{9,3},... | collective-permute-start | bytes 1179656 | tf_op jit(solution)/shard_map/cond/branch_1_fun/ppermute | solution.py:296
  81.1 24.9 %collective-permute-start.27 = (f32[96,1024]{1,0:T(8,128)S(1)}, f32[96,1024]{1,0:T(8,128)S(1)}, u32[]{:S(2)}, u32[]{:S(2)}) collective-permute-start(f32[96,1024]{1,0:T(8,128)S(1)} %select_add_fusion), channel_id=1, source_target_pairs={{0,8},{1,9},{2,10},{3,11},{4,12},{5,13},{6,14},{7,15},{8,0},{9,1},... | collective-permute-start | bytes 1179656 | tf_op jit(solution)/shard_map/cond/branch_1_fun/ppermute | solution.py:296
  81.2 31.4 %collective-permute-start.28 = (f32[96,1024]{1,0:T(8,128)S(1)}, f32[96,1024]{1,0:T(8,128)S(1)}, u32[]{:S(2)}, u32[]{:S(2)}) collective-permute-start(f32[96,1024]{1,0:T(8,128)S(1)} %select_add_fusion), channel_id=1, source_target_pairs={{0,6},{1,7},{2,4},{3,5},{4,2},{5,3},{6,0},{7,1},{8,14},{9,15},{10,... | collective-permute-start | bytes 1179656 | tf_op jit(solution)/shard_map/cond/branch_1_fun/ppermute | solution.py:296
  83.5 29.1 %collective-permute-start.29 = (f32[96,1024]{1,0:T(8,128)S(1)}, f32[96,1024]{1,0:T(8,128)S(1)}, u32[]{:S(2)}, u32[]{:S(2)}) collective-permute-start(f32[96,1024]{1,0:T(8,128)S(1)} %select_add_fusion), channel_id=1, source_target_pairs={{0,4},{1,5},{2,6},{3,7},{4,0},{5,1},{6,2},{7,3},{8,12},{9,13},{10,... | collective-permute-start | bytes 1179656 | tf_op jit(solution)/shard_map/cond/branch_1_fun/ppermute | solution.py:296
  90.4 26.1 %collective-permute-start.30 = (f32[96,1024]{1,0:T(8,128)S(1)}, f32[96,1024]{1,0:T(8,128)S(1)}, u32[]{:S(2)}, u32[]{:S(2)}) collective-permute-start(f32[96,1024]{1,0:T(8,128)S(1)} %select_add_fusion), channel_id=1, source_target_pairs={{0,2},{1,3},{2,0},{3,1},{4,6},{5,7},{6,4},{7,5},{8,10},{9,11},{10,... | collective-permute-start | bytes 1179656 | tf_op jit(solution)/shard_map/cond/branch_1_fun/ppermute | solution.py:296
  98.0 26.2 %collective-permute-start.16 = (f32[96,1024]{1,0:T(8,128)S(1)}, f32[96,1024]{1,0:T(8,128)S(1)}, u32[]{:S(2)}, u32[]{:S(2)}) collective-permute-start(f32[96,1024]{1,0:T(8,128)S(1)} %copy-done.4), channel_id=1, source_target_pairs={{0,112},{16,96},{32,80},{48,64},{64,48},{80,32},{96,16},{112,0},{1... | collective-permute-start | bytes 1179656 | tf_op jit(solution)/shard_map/cond/branch_1_fun/ppermute | solution.py:296
  106.0 28.2 %collective-permute-start.17 = (f32[96,1024]{1,0:T(8,128)S(1)}, f32[96,1024]{1,0:T(8,128)S(1)}, u32[]{:S(2)}, u32[]{:S(2)}) collective-permute-start(f32[96,1024]{1,0:T(8,128)S(1)} %copy-done.4), channel_id=1, source_target_pairs={{0,96},{16,112},{32,64},{48,80},{64,32},{80,48},{96,0},{112,16},{1... | collective-permute-start | bytes 1179656 | tf_op jit(solution)/shard_map/cond/branch_1_fun/ppermute | solution.py:296
  112.6 23.5 %collective-permute-start.18 = (f32[96,1024]{1,0:T(8,128)S(1)}, f32[96,1024]{1,0:T(8,128)S(1)}, u32[]{:S(2)}, u32[]{:S(2)}) collective-permute-start(f32[96,1024]{1,0:T(8,128)S(1)} %copy-done.4), channel_id=1, source_target_pairs={{0,80},{16,64},{32,112},{48,96},{64,16},{80,0},{96,48},{112,32},{1... | collective-permute-start | bytes 1179656 | tf_op jit(solution)/shard_map/cond/branch_1_fun/ppermute | solution.py:296
  112.6 33.0 %collective-permute-start.19 = (f32[96,1024]{1,0:T(8,128)S(1)}, f32[96,1024]{1,0:T(8,128)S(1)}, u32[]{:S(2)}, u32[]{:S(2)}) collective-permute-start(f32[96,1024]{1,0:T(8,128)S(1)} %copy-done.4), channel_id=1, source_target_pairs={{0,64},{16,80},{32,96},{48,112},{64,0},{80,16},{96,32},{112,48},{1... | collective-permute-start | bytes 1179656 | tf_op jit(solution)/shard_map/cond/branch_1_fun/ppermute | solution.py:296
  116.5 32.5 %collective-permute-start.20 = (f32[96,1024]{1,0:T(8,128)S(1)}, f32[96,1024]{1,0:T(8,128)S(1)}, u32[]{:S(2)}, u32[]{:S(2)}) collective-permute-start(f32[96,1024]{1,0:T(8,128)S(1)} %copy-done.4), channel_id=1, source_target_pairs={{0,48},{16,32},{32,16},{48,0},{64,112},{80,96},{96,80},{112,64},{1... | collective-permute-start | bytes 1179656 | tf_op jit(solution)/shard_map/cond/branch_1_fun/ppermute | solution.py:296
  124.2 29.1 %collective-permute-start.21 = (f32[96,1024]{1,0:T(8,128)S(1)}, f32[96,1024]{1,0:T(8,128)S(1)}, u32[]{:S(2)}, u32[]{:S(2)}) collective-permute-start(f32[96,1024]{1,0:T(8,128)S(1)} %copy-done.4), channel_id=1, source_target_pairs={{0,32},{16,48},{32,0},{48,16},{64,96},{80,112},{96,64},{112,80},{1... | collective-permute-start | bytes 1179656 | tf_op jit(solution)/shard_map/cond/branch_1_fun/ppermute | solution.py:296
  134.2 19.2 %collective-permute-start.22 = (f32[96,1024]{1,0:T(8,128)S(1)}, f32[96,1024]{1,0:T(8,128)S(1)}, u32[]{:S(2)}, u32[]{:S(2)}) collective-permute-start(f32[96,1024]{1,0:T(8,128)S(1)} %copy-done.4), channel_id=1, source_target_pairs={{0,16},{16,0},{32,48},{48,32},{64,80},{80,64},{96,112},{112,96},{1... | collective-permute-start | bytes 1179656 | tf_op jit(solution)/shard_map/cond/branch_1_fun/ppermute | solution.py:296
  136.1 65.4 %collective-permute-start.31 = (f32[768,1024]{1,0:T(8,128)}, f32[768,1024]{1,0:T(8,128)}, u32[]{:S(2)}, u32[]{:S(2)}) collective-permute-start(f32[768,1024]{1,0:T(8,128)} %select_dynamic-update-slice_fusion.own_ref), channel_id=1, source_target_pairs={{0,1},{1,0},{2,3},{3,2},{4,5},{5,4},{6,7},{7,6},{8,9},{9,8},{10,11... | collective-permute-start | bytes 9437192 | tf_op jit(solution)/shard_map/cond/branch_1_fun/ppermute | solution.py:288
  145.6 9.2 %collective-permute-start.15 = (f32[768,384]{1,0:T(8,128)S(1)}, f32[768,384]{1,0:T(8,128)S(1)}, u32[]{:S(2)}, u32[]{:S(2)}) collective-permute-start(f32[768,384]{1,0:T(8,128)S(1)} %select_dynamic-update-slice_fusion.16), channel_id=1, source_target_pairs={{0,1},{1,0},{2,3},{3,2},{4,5},{5,4},{6,7},{7,6},{8,9},{9,8},{10,11... | collective-permute-start | bytes 3538952 | tf_op jit(solution)/shard_map/cond/branch_1_fun/ppermute | solution.py:288
  154.7 46.8 %slice-start.2 = ((s8[8388608]{0:T(1024)(128)(4,1)}), s8[4194304]{0:T(1024)(128)(4,1)S(1)}, s32[]{:S(2)}) async-start(s8[8388608]{0:T(1024)(128)(4,1)} %bitcast.65), calls=%async_computation.4 | async-start | bytes 8388608 | tf_op jit(solution)/shard_map/cond
  155.0 46.6 %slice-start.3 = ((s8[8388608]{0:T(1024)(128)(4,1)}), s8[4194304]{0:T(1024)(128)(4,1)S(1)}, s32[]{:S(2)}) async-start(s8[8388608]{0:T(1024)(128)(4,1)} %bitcast.65), calls=%async_computation.5 | async-start | bytes 8388608 | tf_op jit(solution)/shard_map/cond
